TPU v7x, 32 devices: a whole 2x2x4 slice. The times are simulated.
32 devices in a mesh: grp: 2 (over x), obs: 16 (over z, y, core).
Axes of the slice: x: 2, y: 2, z: 4, core: 2. Of those that a mesh axis runs over, the one named last changes fastest.
Arguments:
- anomalies: bfloat16 [512, 16384], P(('grp', 'obs')), parts along dimension 0, may hold values from -6 to 6
- innovations: bfloat16 [512, 16384], P(('grp', 'obs')), parts along dimension 0, may hold values from -6 to 6
- sort_order: int32 [32768], P(('grp', 'obs')), parts along dimension 0, may hold values from 0 to 16383, as said below
- obs_error: float32 [32768], P(('grp', 'obs')), parts along dimension 0, may hold values from 0.2 to 2
Outputs:
- gain_product: float32 [32768, 256], P(('grp', 'obs')), parts along dimension 0
There are 2 independent parts, one for each index of `grp`. A program takes and returns all parts, laid end to end along the dimension named above; each array names one. Nothing has to cross between parts.
Inputs may be any that keep to these rules, and one draw needn't show every extreme that they name: Each acquisition index appears exactly once, and sort_order[p] lies in the same aligned block of 128 positions as p.
All inputs are finite; a program needn't handle non-finite values.
Results may differ from a plain program's by a relative error of at most 0.0025.
Values may be sent and summed in bfloat16 or wider, within the bound.
A program may use at most 64 MiB of HBM per device.

v0:
```python
import jax
import jax.numpy as jnp
from jax import lax
from jax.sharding import PartitionSpec as P


def shifted(shard, axis, by):
    peers = lax.axis_size(axis)
    pairs = [(i, i + by) for i in range(peers) if 0 <= i + by < peers]
    return lax.ppermute(shard, axis, pairs)


def gaspari(z):
    inner = z * z * (z * (z * (-0.25 * z + 0.5) + 0.625) - 5.0 / 3.0) + 1.0
    zs = jnp.maximum(z, 1.0)
    outer = (
        zs * zs * (zs * (zs * (zs / 12.0 - 0.5) + 0.625) + 5.0 / 3.0)
        - 5.0 * zs
        + 4.0
        - 2.0 / (3.0 * zs)
    )
    return jnp.where(z <= 1.0, inner, jnp.where(z < 2.0, outer, 0.0 * z))


def taper_scale(first_row, rows, cols, offset, half_width, members):
    row_ids = first_row + lax.iota(jnp.int32, rows)
    col_ids = lax.iota(jnp.int32, cols) + offset * cols
    dist = jnp.abs(row_ids[:, None] - col_ids[None, :]).astype(jnp.float32)
    return gaspari(dist / half_width) / (members - 1.0)


def permute_blocks(values, selector, width, blocks):
    shaped = values.reshape(values.shape[0], blocks, width)
    moved = jnp.einsum("mbi,bij->mbj", shaped, selector, preferred_element_type=jnp.float32)
    return moved.astype(jnp.bfloat16).reshape(values.shape[0], blocks * width)


def on_device(anomalies, innovations, sort_order, obs_error):
    raw_y, raw_d = (
        lax.all_to_all(anomalies, "obs", split_axis=1, concat_axis=0, tiled=True),
        lax.all_to_all(innovations, "obs", split_axis=1, concat_axis=0, tiled=True),
    )
    members = raw_y.shape[0]
    panel = raw_y.shape[1]
    width = min(128, panel)
    blocks = panel // width
    local_ids = (sort_order % width).reshape(blocks, width)
    selector = (lax.iota(jnp.int32, width)[None, :, None] == local_ids[:, None, :]).astype(
        jnp.bfloat16
    )
    y_here = permute_blocks(raw_y, selector, width, blocks)
    d_here = permute_blocks(raw_d, selector, width, blocks)
    block = min(512, panel)
    half_width = panel // 2 * 1.0

    def tile_rows(first, y_cols, offset):
        row_part = lax.slice_in_dim(y_here, first, first + block, axis=1)
        gram = lax.dot_general(
            row_part, y_cols, (((0,), (0,)), ((), ())), preferred_element_type=jnp.float32
        )
        return (gram * taper_scale(first, block, panel, offset, half_width, members * 1.0)).astype(
            jnp.bfloat16
        )

    def apply_rows(weights, d_cols):
        return lax.dot_general(
            weights, d_cols, (((1,), (1,)), ((), ())), preferred_element_type=jnp.float32
        )

    pieces = []
    low_y, low_d = shifted((y_here, d_here), "obs", 1)
    up_y, up_d = shifted((y_here, d_here), "obs", -1)
    for first in range(0, panel, block):
        acc = apply_rows(tile_rows(first, y_here, 0), d_here)
        acc = acc + apply_rows(tile_rows(first, low_y, -1), low_d)
        acc = acc + apply_rows(tile_rows(first, up_y, 1), up_d)
        pieces.append(acc)
    total = jnp.concatenate(pieces, axis=0)
    return total + obs_error[:, None] * d_here.T.astype(jnp.float32)


def solution(mesh):
    return jax.shard_map(
        on_device,
        mesh=mesh,
        in_specs=(
            P(("grp", "obs"), None),
            P(("grp", "obs"), None),
            P(("grp", "obs")),
            P(("grp", "obs")),
        ),
        out_specs=P(("grp", "obs"), None),
        check_vma=False,
    )
```

profile of v0, /device:TPU:14, one launch (start us, length us, event | category | flops | bytes accessed | tf_op | source)
XLA Modules:
  0.0 76.1 jit_solution(12527095984979136979)
XLA Ops:
  0.0 0.0 copy-start
  0.0 1.9 %copy.19 = bf16[2,16,8,1024]{3,2,0,1:T(8,128)(2,1)} copy(bf16[2,16,8,1024]{3,2,1,0:T(8,128)(2,1)} %bitcast.47) | data formatting | bytes 1048576 | tf_op jit(solution)/shard_map/all_to_all | solution.py:41
  1.9 6.2 %all-to-all-start.1 = ((bf16[16,16,1024]{2,0,1:T(8,128)(2,1)}), bf16[16,16,1024]{2,0,1:T(8,128)(2,1)S(1)}, u32[]{:S(2)}, u32[]{:S(2)}) async-start(bf16[16,16,1024]{2,0,1:T(8,128)(2,1)} %bitcast.37), calls=%async_computation.1 | async-start | bytes 1048576 | tf_op jit(solution)/shard_map/all_to_all | solution.py:41
  8.2 0.0 copy-done
  8.2 0.0 copy-start.2
  8.2 0.8 %copy.20 = bf16[2,16,8,1024]{3,2,0,1:T(8,128)(2,1)} copy(bf16[2,16,8,1024]{3,2,1,0:T(8,128)(2,1)S(1)} %bitcast.48) | data formatting | bytes 1048576 | tf_op jit(solution)/shard_map/all_to_all | solution.py:40
  9.0 12.6 %all-to-all-done.1 = bf16[16,16,1024]{2,0,1:T(8,128)(2,1)S(1)} async-done(((bf16[16,16,1024]{2,0,1:T(8,128)(2,1)}), bf16[16,16,1024]{2,0,1:T(8,128)(2,1)S(1)}, u32[]{:S(2)}, u32[]{:S(2)}) %all-to-all-start.1) | async-done | bytes 524320 | tf_op jit(solution)/shard_map/all_to_all | solution.py:41
  21.6 5.1 %all-to-all-start = ((bf16[16,16,1024]{2,0,1:T(8,128)(2,1)}), bf16[16,16,1024]{2,0,1:T(8,128)(2,1)S(1)}, u32[]{:S(2)}, u32[]{:S(2)}) async-start(bf16[16,16,1024]{2,0,1:T(8,128)(2,1)} %bitcast.38), calls=%async_computation | async-start | bytes 1048576 | tf_op jit(solution)/shard_map/all_to_all | solution.py:40
  26.8 0.0 copy-done.2
  26.8 0.1 copy.12
  26.9 0.3 convolution_convert_fusion
  27.3 2.1 %collective-permute-start.1 = (bf16[256,1024]{0,1:T(8,128)(2,1)S(1)}, bf16[256,1024]{0,1:T(8,128)(2,1)S(1)}, u32[]{:S(2)}, u32[]{:S(2)}) collective-permute-start(bf16[256,1024]{0,1:T(8,128)(2,1)S(1)} %bitcast.39), channel_id=1, source_target_pairs={{0,1},{1,2},{2,3},{3,4},{4,5},{5,6},{6,7},{7,8},{8,9},{9,10},{10,1... | collective-permute-start | bytes 1572872 | tf_op jit(solution)/shard_map/ppermute | solution.py:10
  29.3 3.5 %collective-permute-start.3 = (bf16[256,1024]{0,1:T(8,128)(2,1)S(1)}, bf16[256,1024]{0,1:T(8,128)(2,1)S(1)}, u32[]{:S(2)}, u32[]{:S(2)}) collective-permute-start(bf16[256,1024]{0,1:T(8,128)(2,1)S(1)} %bitcast.40), channel_id=1, source_target_pairs={{1,0},{2,1},{3,2},{4,3},{5,4},{6,5},{7,6},{8,7},{9,8},{10,9},{11,1... | collective-permute-start | bytes 1572872 | tf_op jit(solution)/shard_map/ppermute | solution.py:10
  32.8 7.4 %all-to-all-done = bf16[16,16,1024]{2,0,1:T(8,128)(2,1)S(1)} async-done(((bf16[16,16,1024]{2,0,1:T(8,128)(2,1)}), bf16[16,16,1024]{2,0,1:T(8,128)(2,1)S(1)}, u32[]{:S(2)}, u32[]{:S(2)}) %all-to-all-start) | async-done | bytes 524320 | tf_op jit(solution)/shard_map/all_to_all | solution.py:40
  40.2 0.1 copy.11
  40.3 0.3 convolution_convert_fusion.1
  40.6 2.5 %collective-permute-start = (bf16[256,1024]{0,1:T(8,128)(2,1)S(1)}, bf16[256,1024]{0,1:T(8,128)(2,1)S(1)}, u32[]{:S(2)}, u32[]{:S(2)}) collective-permute-start(bf16[256,1024]{0,1:T(8,128)(2,1)S(1)} %bitcast.49), channel_id=1, source_target_pairs={{0,1},{1,2},{2,3},{3,4},{4,5},{5,6},{6,7},{7,8},{8,9},{9,10},{10,1... | collective-permute-start | bytes 1572872 | tf_op jit(solution)/shard_map/ppermute | solution.py:10
  43.2 3.1 %collective-permute-start.2 = (bf16[256,1024]{0,1:T(8,128)(2,1)S(1)}, bf16[256,1024]{0,1:T(8,128)(2,1)}, u32[]{:S(2)}, u32[]{:S(2)}) collective-permute-start(bf16[256,1024]{0,1:T(8,128)(2,1)S(1)} %bitcast.50), channel_id=1, source_target_pairs={{1,0},{2,1},{3,2},{4,3},{5,4},{6,5},{7,6},{8,7},{9,8},{10,9},{11,1... | collective-permute-start | bytes 1572872 | tf_op jit(solution)/shard_map/ppermute | solution.py:10
  46.2 3.8 %fusion.7 = f32[512,256]{1,0:T(8,128)} fusion(bf16[256,1024]{0,1:T(8,128)(2,1)S(1)} %bitcast.41, bf16[256,1024]{0,1:T(8,128)(2,1)S(1)} %bitcast.51, s32[512]{0:T(512)S(1)} %iota_add_fusion.2), kind=kOutput, calls=%fused_computation.43 | convolution fusion | flops 555745280 | bytes 1837056 | tf_op jit(solution)/shard_map/dot_general | solution.py:66
  50.0 2.8 %fusion.6 = f32[512,256]{1,0:T(8,128)S(1)} fusion(bf16[256,1024]{0,1:T(8,128)(2,1)S(1)} %bitcast.42, bf16[256,1024]{0,1:T(8,128)(2,1)S(1)} %bitcast.52), kind=kOutput, calls=%fused_computation.42 | convolution fusion | flops 555745280 | bytes 1835008 | tf_op jit(solution)/shard_map/dot_general | solution.py:66
  52.7 0.0 collective-permute-done.1
  52.7 5.3 %collective-permute-done = bf16[256,1024]{0,1:T(8,128)(2,1)S(1)} collective-permute-done((bf16[256,1024]{0,1:T(8,128)(2,1)S(1)}, bf16[256,1024]{0,1:T(8,128)(2,1)S(1)}, u32[]{:S(2)}, u32[]{:S(2)}) %collective-permute-start) | collective-permute-done | bytes 524320 | tf_op jit(solution)/shard_map/ppermute | solution.py:10
  58.1 4.8 %convolution_add_fusion.1 = f32[512,256]{1,0:T(8,128)} fusion(f32[512,256]{1,0:T(8,128)} %fusion.7, bf16[256,1024]{0,1:T(8,128)(2,1)S(1)} %collective-permute-done.1, bf16[256,1024]{0,1:T(8,128)(2,1)S(1)} %collective-permute-done, s32[512]{0:T(512)S(1)} %iota_add_fusion.2, s32[1024]{0:T(1024)S(1)} %iota_add_fusion.1, bf16[256,1024]{0,1:T(8,128)(2,1)S(1)} %bitcast.53), kind=kOutput, calls=%fused_computation.39 | convolution fusion | flops 555876352 | bytes 2365440 | tf_op jit(solution)/shard_map/dot_general | solution.py:66
  62.9 3.7 %convolution_add_fusion.3 = f32[512,256]{1,0:T(8,128)} fusion(f32[512,256]{1,0:T(8,128)S(1)} %fusion.6, bf16[256,1024]{0,1:T(8,128)(2,1)S(1)} %collective-permute-done.1, bf16[256,1024]{0,1:T(8,128)(2,1)S(1)} %collective-permute-done, s32[1024]{0:T(1024)S(1)} %iota_add_fusion.1, bf16[256,1024]{0,1:T(8,128)(2,1)S(1)} %bitcast.54), kind=kOutput, calls=%fused_computation.41 | convolution fusion | flops 555876352 | bytes 2363392 | tf_op jit(solution)/shard_map/dot_general | solution.py:66
  66.6 0.0 copy-start.3
  66.6 0.0 collective-permute-done.3
  66.6 0.0 collective-permute-done.2
  66.6 4.4 %convolution_add_fusion = f32[512,256]{1,0:T(8,128)S(1)} fusion(f32[512,256]{1,0:T(8,128)} %convolution_add_fusion.1, bf16[256,1024]{0,1:T(8,128)(2,1)S(1)} %collective-permute-done.3, bf16[256,1024]{0,1:T(8,128)(2,1)} %collective-permute-done.2, s32[512]{0:T(512)S(1)} %iota_add_fusion.2, s32[1024]{0:T(1024)S(1)} %iota_add_fusion, ...), kind=kOutput, calls=%fused_computation.38 | convolution fusion | flops 555876352 | bytes 2365440 | tf_op jit(solution)/shard_map/dot_general | solution.py:66
  70.9 0.0 copy-done.3
  70.9 0.0 copy-start.1
  70.9 4.0 %convolution_add_fusion.2 = f32[512,256]{1,0:T(8,128)S(1)} fusion(f32[512,256]{1,0:T(8,128)S(1)} %copy-done.3, bf16[256,1024]{0,1:T(8,128)(2,1)S(1)} %collective-permute-done.3, bf16[256,1024]{0,1:T(8,128)(2,1)} %collective-permute-done.2, s32[1024]{0:T(1024)S(1)} %iota_add_fusion, bf16[256,1024]{0,1:T(8,128)(2,1)S(1)} %bitcast.56), kind=kOutput, calls=%fused_computation.40 | convolution fusion | flops 555876352 | bytes 2363392 | tf_op jit(solution)/shard_map/dot_general | solution.py:66
  74.9 0.0 copy-done.1
  74.9 1.2 %maximum_add_fusion = f32[1024,256]{1,0:T(8,128)} fusion(f32[512,256]{1,0:T(8,128)S(1)} %convolution_add_fusion, f32[512,256]{1,0:T(8,128)S(1)} %convolution_add_fusion.2, f32[1024]{0:T(1024)S(1)} %copy-done.1, bf16[8,128,256]{2,1,0:T(8,128)(2,1)S(1)} %convolution_convert_fusion), kind=kLoop, calls=%fused_computation.44 | loop fusion | flops 1048576 | bytes 2625536 | tf_op jit(solution)/shard_map/add | solution.py:79
  (4 shorter events, 0.0 us)
Async XLA Ops:
  0.0 8.2 %copy-start = (bf16[16,16384]{1,0:T(8,128)(2,1)S(1)}, bf16[16,16384]{1,0:T(8,128)(2,1)}, u32[]{:S(2)}) copy-start(bf16[16,16384]{1,0:T(8,128)(2,1)} %param.4) | copy-start | bytes 1572868
  1.9 19.7 %all-to-all-start.1 = ((bf16[16,16,1024]{2,0,1:T(8,128)(2,1)}), bf16[16,16,1024]{2,0,1:T(8,128)(2,1)S(1)}, u32[]{:S(2)}, u32[]{:S(2)}) async-start(bf16[16,16,1024]{2,0,1:T(8,128)(2,1)} %bitcast.37), calls=%async_computation.1 | async-start | bytes 1048576 | tf_op jit(solution)/shard_map/all_to_all | solution.py:41
  8.2 18.6 %copy-start.2 = (s32[1024]{0:T(1024)S(1)}, s32[1024]{0:T(1024)}, u32[]{:S(2)}) copy-start(s32[1024]{0:T(1024)} %param.6) | copy-start | bytes 12292
  21.6 18.6 %all-to-all-start = ((bf16[16,16,1024]{2,0,1:T(8,128)(2,1)}), bf16[16,16,1024]{2,0,1:T(8,128)(2,1)S(1)}, u32[]{:S(2)}, u32[]{:S(2)}) async-start(bf16[16,16,1024]{2,0,1:T(8,128)(2,1)} %bitcast.38), calls=%async_computation | async-start | bytes 1048576 | tf_op jit(solution)/shard_map/all_to_all | solution.py:40
  27.3 25.5 %collective-permute-start.1 = (bf16[256,1024]{0,1:T(8,128)(2,1)S(1)}, bf16[256,1024]{0,1:T(8,128)(2,1)S(1)}, u32[]{:S(2)}, u32[]{:S(2)}) collective-permute-start(bf16[256,1024]{0,1:T(8,128)(2,1)S(1)} %bitcast.39), channel_id=1, source_target_pairs={{0,1},{1,2},{2,3},{3,4},{4,5},{5,6},{6,7},{7,8},{8,9},{9,10},{10,1... | collective-permute-start | bytes 1572872 | tf_op jit(solution)/shard_map/ppermute | solution.py:10
  29.3 37.2 %collective-permute-start.3 = (bf16[256,1024]{0,1:T(8,128)(2,1)S(1)}, bf16[256,1024]{0,1:T(8,128)(2,1)S(1)}, u32[]{:S(2)}, u32[]{:S(2)}) collective-permute-start(bf16[256,1024]{0,1:T(8,128)(2,1)S(1)} %bitcast.40), channel_id=1, source_target_pairs={{1,0},{2,1},{3,2},{4,3},{5,4},{6,5},{7,6},{8,7},{9,8},{10,9},{11,1... | collective-permute-start | bytes 1572872 | tf_op jit(solution)/shard_map/ppermute | solution.py:10
  40.6 17.4 %collective-permute-start = (bf16[256,1024]{0,1:T(8,128)(2,1)S(1)}, bf16[256,1024]{0,1:T(8,128)(2,1)S(1)}, u32[]{:S(2)}, u32[]{:S(2)}) collective-permute-start(bf16[256,1024]{0,1:T(8,128)(2,1)S(1)} %bitcast.49), channel_id=1, source_target_pairs={{0,1},{1,2},{2,3},{3,4},{4,5},{5,6},{6,7},{7,8},{8,9},{9,10},{10,1... | collective-permute-start | bytes 1572872 | tf_op jit(solution)/shard_map/ppermute | solution.py:10
  43.2 23.4 %collective-permute-start.2 = (bf16[256,1024]{0,1:T(8,128)(2,1)S(1)}, bf16[256,1024]{0,1:T(8,128)(2,1)}, u32[]{:S(2)}, u32[]{:S(2)}) collective-permute-start(bf16[256,1024]{0,1:T(8,128)(2,1)S(1)} %bitcast.50), channel_id=1, source_target_pairs={{1,0},{2,1},{3,2},{4,3},{5,4},{6,5},{7,6},{8,7},{9,8},{10,9},{11,1... | collective-permute-start | bytes 1572872 | tf_op jit(solution)/shard_map/ppermute | solution.py:10
  66.6 4.4 %copy-start.3 = (f32[512,256]{1,0:T(8,128)S(1)}, f32[512,256]{1,0:T(8,128)}, u32[]{:S(2)}) copy-start(f32[512,256]{1,0:T(8,128)} %convolution_add_fusion.3) | copy-start | bytes 1572868
  70.9 4.0 %copy-start.1 = (f32[1024]{0:T(1024)S(1)}, f32[1024]{0:T(1024)}, u32[]{:S(2)}) copy-start(f32[1024]{0:T(1024)} %param.7) | copy-start | bytes 12292
where the time goes:
time: 76.6 us; the launch traced here: 76.1 us
  waiting for transfers between devices  25.3 us (33%)
  matrix products  24 us (31%)
  starting transfers between devices  22.5 us (29%)
  local copies, waits for them, and re-layouts  2.97 us (4%)
  other arithmetic  1.21 us (2%)
    dot_general x6, matrix products, apply_rows(): lax.dot_general(weights, d_cols, (((1,), (1,)), ((), ())), preferred_elem...  23.3 us
    all_to_all x1, waiting for transfers between devices, on_device(): lax.all_to_all(innovations, 'obs', split_axis=1, concat_axis=0, tiled=True)  12.6 us
    ppermute x4, starting transfers between devices, shifted(): return lax.ppermute(shard, axis, pairs)  11.1 us
    all_to_all x1, waiting for transfers between devices, on_device(): lax.all_to_all(anomalies, 'obs', split_axis=1, concat_axis=0, tiled=True)  7.37 us
    all_to_all x1, starting transfers between devices, on_device(): lax.all_to_all(innovations, 'obs', split_axis=1, concat_axis=0, tiled=True)  6.24 us
    ppermute x4, waiting for transfers between devices, shifted(): return lax.ppermute(shard, axis, pairs)  5.34 us
    all_to_all x1, starting transfers between devices, on_device(): lax.all_to_all(anomalies, 'obs', split_axis=1, concat_axis=0, tiled=True)  5.13 us
    all_to_all x1, local copies, waits for them, and re-layouts, on_device(): lax.all_to_all(innovations, 'obs', split_axis=1, concat_axis=0, tiled=True)  1.93 us
  transfers between devices with their start and end apart: 6, of which 3 were waited for; matrix products, arithmetic and copies ran while one was open for 22% of the time, Pallas kernels for 0%

commit v1 on v0

--- a/solution.py
+++ b/solution.py
@@ -1,6 +1,10 @@
+import functools
+
 import jax
 import jax.numpy as jnp
 from jax import lax
+from jax.experimental import pallas as pl
+from jax.experimental.pallas import tpu as pltpu
 from jax.sharding import PartitionSpec as P
 
 
@@ -35,7 +39,7 @@
     return moved.astype(jnp.bfloat16).reshape(values.shape[0], blocks * width)
 
 
-def on_device(anomalies, innovations, sort_order, obs_error):
+def plain_on_device(anomalies, innovations, sort_order, obs_error):
     raw_y, raw_d = (
         lax.all_to_all(anomalies, "obs", split_axis=1, concat_axis=0, tiled=True),
         lax.all_to_all(innovations, "obs", split_axis=1, concat_axis=0, tiled=True),
@@ -79,9 +83,255 @@
     return total + obs_error[:, None] * d_here.T.astype(jnp.float32)
 
 
+TILE = 256
+SORT = 128
+MESH = pl.DeviceIdType.MESH
+NT = (((1,), (1,)), ((), ()))
+NN = (((1,), (0,)), ((), ()))
+
+
+def mm(a, b, dims=NN):
+    return lax.dot_general(a, b, dims, preferred_element_type=jnp.float32)
+
+
+def target_order(n):
+    half = n // 2
+    order = [half]
+    for step in range(1, half):
+        order += [half + step, half - step]
+    return order
+
+
+def kernel(
+    n, parts,
+    y_any, d_any, order_ref, err_ref, out_ref,
+    raw, y_ext, d_ext, y_t, weights, table, sel, sel_t, err_col,
+    send_sem, recv_sem, own_sem, hsend_sem, hrecv_sem,
+):
+    me = lax.axis_index("obs")
+    rows = y_any.shape[0]
+    panel = y_any.shape[1] // n
+    members = rows * n
+    tiles = panel // TILE
+    width = panel // parts
+    has_low, has_up = me > 0, me < n - 1
+    chunks = [(a, c) for a in range(2) for c in range(parts)]
+
+    barrier = pltpu.get_barrier_semaphore()
+    for k in range(1, n):
+        pl.semaphore_signal(
+            barrier, inc=1, device_id={"obs": lax.rem(me + k, n)}, device_id_type=MESH
+        )
+    pl.semaphore_wait(barrier, n - 1)
+
+    def member_copy(i, k, owner, source):
+        a, c = chunks[i]
+        start = pl.multiple_of(owner * panel + c * width, SORT)
+        return pltpu.make_async_remote_copy(
+            src_ref=(y_any, d_any)[a].at[:, pl.ds(start, width)],
+            dst_ref=raw.at[a, source, :, pl.ds(c * width, width)],
+            send_sem=send_sem.at[i, k],
+            recv_sem=recv_sem.at[i, k],
+            device_id={"obs": owner},
+            device_id_type=MESH,
+        )
+
+    def own_copy(a):
+        start = pl.multiple_of(me * panel, SORT)
+        return pltpu.make_async_copy(
+            (y_any, d_any)[a].at[:, pl.ds(start, panel)], raw.at[a, me], own_sem.at[a]
+        )
+
+    def panel_copy(i, up):
+        a, c = chunks[i]
+        ext = (y_ext, d_ext)[a]
+        here = pl.ds(panel + c * width, width)
+        there = pl.ds((0 if up else 2 * panel) + c * width, width)
+        src, dst = (ext.at[:, here], ext.at[:, there]) if a == 0 else (ext.at[here], ext.at[there])
+        return pltpu.make_async_remote_copy(
+            src_ref=src,
+            dst_ref=dst,
+            send_sem=hsend_sem.at[i, up],
+            recv_sem=hrecv_sem.at[i, up],
+            device_id={"obs": lax.rem(me + (1 if up else n - 1), n)},
+            device_id_type=MESH,
+        )
+
+    for i in range(len(chunks)):
+        for k in target_order(n):
+            member_copy(i, k, lax.rem(me + k, n), me).start()
+    for a in range(2):
+        own_copy(a).start()
+
+    row_id = lax.broadcasted_iota(jnp.int32, (SORT, SORT), 0)
+    col_id = lax.broadcasted_iota(jnp.int32, (SORT, SORT), 1)
+    for b in range(panel // SORT):
+        ids = jnp.broadcast_to(order_ref[b : b + 1, :] & (SORT - 1), (SORT, SORT))
+        pick = (row_id == ids).astype(jnp.float32)
+        sel[b] = pick.astype(jnp.bfloat16)
+        sel_t[b] = pick.T.astype(jnp.bfloat16)
+        err = jnp.broadcast_to(err_ref[b : b + 1, :], (SORT, SORT))
+        column = jnp.sum(jnp.where(row_id == col_id, err, 0.0), axis=1, keepdims=True)
+        err_col[b * SORT : (b + 1) * SORT, :] = jnp.broadcast_to(column, (SORT, SORT))
+    r = lax.broadcasted_iota(jnp.int32, (TILE, TILE), 0)
+    s = lax.broadcasted_iota(jnp.int32, (TILE, TILE), 1)
+    for j in range(2 * tiles + 1):
+        dist = jnp.abs(s - r + (j - tiles) * TILE).astype(jnp.float32)
+        table[:, j * TILE : (j + 1) * TILE] = gaspari(dist / (panel // 2 * 1.0)) / (
+            members - 1.0
+        )
+
+    def make_weights(j):
+        for t in range(tiles):
+            at = j - t
+            if 0 <= at <= 2 * tiles:
+                cols = slice(at * TILE, (at + 1) * TILE)
+                gram = mm(y_t[t * TILE : (t + 1) * TILE, :], y_ext[:, j * TILE : (j + 1) * TILE])
+                weights[t, :, cols] = (gram * table[:, cols]).astype(jnp.bfloat16)
+
+    def apply_weights(first, last):
+        for t in range(tiles):
+            lo, hi = max(first, t), min(last, t + 2 * tiles + 1)
+            if lo < hi:
+                term = mm(
+                    weights[t, :, (lo - t) * TILE : (hi - t) * TILE],
+                    d_ext[lo * TILE : hi * TILE, :],
+                )
+                here = slice(t * TILE, (t + 1) * TILE)
+                out_ref[here, :] = out_ref[here, :] + term
+
+    def sort_chunk(i):
+        a, c = chunks[i]
+        for k in target_order(n):
+            member_copy(i, k, me, lax.rem(me + n - k, n)).wait_recv()
+        for b in range(c * width // SORT, (c + 1) * width // SORT):
+            cols = slice(b * SORT, (b + 1) * SORT)
+            ext_at = slice(panel + b * SORT, panel + (b + 1) * SORT)
+            block = raw[a, :, :, cols].reshape(members, SORT)
+            turned = mm(sel_t[b], block, NT)
+            if a == 0:
+                y_ext[:, ext_at] = mm(block, sel[b]).astype(jnp.bfloat16)
+                y_t[cols, :] = turned.astype(jnp.bfloat16)
+            else:
+                d_ext[ext_at, :] = turned.astype(jnp.bfloat16)
+                out_ref[cols, :] = err_col[cols, 0:1] * turned
+
+    def send_panels(i):
+        @pl.when(has_up)
+        def _():
+            panel_copy(i, 1).start()
+
+        @pl.when(has_low)
+        def _():
+            panel_copy(i, 0).start()
+
+    for a in range(2):
+        own_copy(a).wait()
+    for i in range(parts):
+        sort_chunk(i)
+        send_panels(i)
+    for j in range(tiles, 2 * tiles):
+        make_weights(j)
+    for i in range(parts):
+        @pl.when(has_low)
+        def _():
+            panel_copy(i, 1).wait_recv()
+
+        @pl.when(has_up)
+        def _():
+            panel_copy(i, 0).wait_recv()
+
+    @pl.when(has_low)
+    def _():
+        for j in range(tiles):
+            make_weights(j)
+
+    @pl.when(has_up)
+    def _():
+        for j in range(2 * tiles, 3 * tiles):
+            make_weights(j)
+
+    for i in range(parts, 2 * parts):
+        sort_chunk(i)
+        send_panels(i)
+    apply_weights(tiles, 2 * tiles)
+
+    @pl.when(has_low)
+    def _():
+        for i in range(parts, 2 * parts):
+            panel_copy(i, 1).wait_recv()
+        apply_weights(0, tiles)
+
+    @pl.when(has_up)
+    def _():
+        for i in range(parts, 2 * parts):
+            panel_copy(i, 0).wait_recv()
+        apply_weights(2 * tiles, 3 * tiles)
+
+    for i in range(len(chunks)):
+        for k in target_order(n):
+            member_copy(i, k, lax.rem(me + k, n), me).wait_send()
+
+        @pl.when(has_up)
+        def _():
+            panel_copy(i, 1).wait_send()
+
+        @pl.when(has_low)
+        def _():
+            panel_copy(i, 0).wait_send()
+
+
+def fused_on_device(n, anomalies, innovations, sort_order, obs_error):
+    rows, total = anomalies.shape
+    panel = total // n
+    members = rows * n
+    parts = 2
+    tiles = panel // TILE
+    bf16, f32 = jnp.bfloat16, jnp.float32
+    vmem = pl.BlockSpec(memory_space=pltpu.VMEM)
+    hbm = pl.BlockSpec(memory_space=pl.ANY)
+    return pl.pallas_call(
+        functools.partial(kernel, n, parts),
+        out_shape=jax.ShapeDtypeStruct((panel, members), f32),
+        in_specs=[hbm, hbm, vmem, vmem],
+        out_specs=vmem,
+        scratch_shapes=[
+            pltpu.VMEM((2, n, rows, panel), bf16),
+            pltpu.VMEM((members, 3 * panel), bf16),
+            pltpu.VMEM((3 * panel, members), bf16),
+            pltpu.VMEM((panel, members), bf16),
+            pltpu.VMEM((tiles, TILE, (2 * tiles + 1) * TILE), bf16),
+            pltpu.VMEM((TILE, (2 * tiles + 1) * TILE), f32),
+            pltpu.VMEM((panel // SORT, SORT, SORT), bf16),
+            pltpu.VMEM((panel // SORT, SORT, SORT), bf16),
+            pltpu.VMEM((panel, SORT), f32),
+            pltpu.SemaphoreType.DMA((2 * parts, n)),
+            pltpu.SemaphoreType.DMA((2 * parts, n)),
+            pltpu.SemaphoreType.DMA((2,)),
+            pltpu.SemaphoreType.DMA((2 * parts, 2)),
+            pltpu.SemaphoreType.DMA((2 * parts, 2)),
+        ],
+        compiler_params=pltpu.CompilerParams(
+            collective_id=0, has_side_effects=True, vmem_limit_bytes=48 * 1024 * 1024
+        ),
+    )(
+        anomalies,
+        innovations,
+        sort_order.reshape(panel // SORT, SORT),
+        obs_error.reshape(panel // SORT, SORT),
+    )
+
+
+def on_device(n, anomalies, innovations, sort_order, obs_error):
+    rows, total = anomalies.shape
+    if rows % 16 or (total // n) % (2 * TILE) or (rows * n) % TILE:
+        return plain_on_device(anomalies, innovations, sort_order, obs_error)
+    return fused_on_device(n, anomalies, innovations, sort_order, obs_error)
+
+
 def solution(mesh):
     return jax.shard_map(
-        on_device,
+        functools.partial(on_device, mesh.shape["obs"]),
         mesh=mesh,
         in_specs=(
             P(("grp", "obs"), None),

time: 76.6 us -> 55.9 us (0.73)
  Pallas kernels: 0 us -> 51.2 us
  waiting for transfers between devices: 25.3 us -> 0 us
  matrix products: 24 us -> 0 us
  starting transfers between devices: 22.5 us -> 0 us
  local copies, waits for them, and re-layouts: 2.97 us -> 4.43 us
  other arithmetic: 1.21 us -> 0 us
    pallas_call x0 -> x1, Pallas kernels: none -> 51.2 us  [fused_on_device(): pl.pallas_call(functools.partial(kernel, n, parts), out_shape=jax.ShapeDt...]
    dot_general x8 -> x0, matrix products: 24 us -> none  [the longest x6 23.3 us: apply_rows(): lax.dot_general(weights, d_cols, (((1,), (1,)), ((), ())), preferred_elem...]
    all_to_all x2 -> x0, waiting for transfers between devices: 20 us -> none  [the longest x1 12.6 us: on_device(): lax.all_to_all(innovations, 'obs', split_axis=1, concat_axis=0, tiled=True)]
    all_to_all x2 -> x0, starting transfers between devices: 11.4 us -> none  [the longest x1 6.24 us: on_device(): lax.all_to_all(innovations, 'obs', split_axis=1, concat_axis=0, tiled=True)]
    ppermute x4 -> x0, starting transfers between devices: 11.1 us -> none  [shifted(): return lax.ppermute(shard, axis, pairs)]
    ppermute x4 -> x0, waiting for transfers between devices: 5.34 us -> none  [shifted(): return lax.ppermute(shard, axis, pairs)]
    unnamed x10 -> x9, local copies, waits for them, and re-layouts: 0.2 us -> 4.43 us
    all_to_all x2 -> x0, local copies, waits for them, and re-layouts: 2.77 us -> none  [the longest x1 1.93 us: on_device(): lax.all_to_all(innovations, 'obs', split_axis=1, concat_axis=0, tiled=True)]
  transfers between devices with their start and end apart: 6 -> 0, of which waited for: 3 -> 0; matrix products, arithmetic and copies ran while one was open for 22% -> 0% of each run, Pallas kernels for 0% -> 0%
where the time goes in v1:
time: 55.9 us; the launch traced here: 55.7 us
  Pallas kernels  51.2 us (92%)
  local copies, waits for them, and re-layouts  4.43 us (8%)
    pallas_call x1, Pallas kernels, fused_on_device(): pl.pallas_call(functools.partial(kernel, n, parts), out_shape=jax.ShapeDt...  51.2 us
    unnamed x9, local copies, waits for them, and re-layouts  4.43 us

profile of v1, /device:TPU:14, one launch (start us, length us, event | category | flops | bytes accessed | tf_op | source)
XLA Modules:
  0.0 55.7 jit_solution(10657760836286869746)
XLA Ops:
  0.0 0.0 copy-start
  0.0 1.0 %copy-done = bf16[16,16384]{1,0:T(8,128)(2,1)S(1)} copy-done((bf16[16,16384]{1,0:T(8,128)(2,1)S(1)}, bf16[16,16384]{1,0:T(8,128)(2,1)}, u32[]{:S(2)}) %copy-start) | copy-done | bytes 524312
  1.0 0.0 copy-start.1
  1.0 1.0 %copy-done.1 = bf16[16,16384]{1,0:T(8,128)(2,1)S(1)} copy-done((bf16[16,16384]{1,0:T(8,128)(2,1)S(1)}, bf16[16,16384]{1,0:T(8,128)(2,1)}, u32[]{:S(2)}) %copy-start.1) | copy-done | bytes 524312
  2.1 0.0 copy-start.2
  2.1 0.7 %copy-done.2 = s32[1024]{0:T(1024)S(1)} copy-done((s32[1024]{0:T(1024)S(1)}, s32[1024]{0:T(1024)}, u32[]{:S(2)}) %copy-start.2) | copy-done | bytes 4120
  2.8 0.0 copy-start.3
  2.8 0.7 %copy-done.3 = f32[1024]{0:T(1024)S(1)} copy-done((f32[1024]{0:T(1024)S(1)}, f32[1024]{0:T(1024)}, u32[]{:S(2)}) %copy-start.3) | copy-done | bytes 4120
  3.5 51.2 %shard_map.46 = f32[1024,256]{1,0:T(8,128)S(1)} custom-call(bf16[16,16384]{1,0:T(8,128)(2,1)S(1)} %copy-done, bf16[16,16384]{1,0:T(8,128)(2,1)S(1)} %copy-done.1, s32[8,128]{1,0:T(8,128)S(1)} %bitcast.2, f32[8,128]{1,0:T(8,128)S(1)} %bitcast.3), custom_call_target="tpu_custom_call" | custom-call | tf_op jit(solution)/shard_map/pallas_call | solution.py:293
  54.7 1.0 %copy.6 = f32[1024,256]{1,0:T(8,128)} copy(f32[1024,256]{1,0:T(8,128)S(1)} %shard_map.46) | data formatting | bytes 2097152
Async XLA Ops:
  0.0 1.0 %copy-start = (bf16[16,16384]{1,0:T(8,128)(2,1)S(1)}, bf16[16,16384]{1,0:T(8,128)(2,1)}, u32[]{:S(2)}) copy-start(bf16[16,16384]{1,0:T(8,128)(2,1)} %y_any.1) | copy-start | bytes 1572868
  1.0 1.0 %copy-start.1 = (bf16[16,16384]{1,0:T(8,128)(2,1)S(1)}, bf16[16,16384]{1,0:T(8,128)(2,1)}, u32[]{:S(2)}) copy-start(bf16[16,16384]{1,0:T(8,128)(2,1)} %d_any.1) | copy-start | bytes 1572868
  2.1 0.7 %copy-start.2 = (s32[1024]{0:T(1024)S(1)}, s32[1024]{0:T(1024)}, u32[]{:S(2)}) copy-start(s32[1024]{0:T(1024)} %param.6) | copy-start | bytes 12292
  2.8 0.7 %copy-start.3 = (f32[1024]{0:T(1024)S(1)}, f32[1024]{0:T(1024)}, u32[]{:S(2)}) copy-start(f32[1024]{0:T(1024)} %param.7) | copy-start | bytes 12292

commit v2 on v0

--- a/solution.py
+++ b/solution.py
@@ -1,6 +1,10 @@
+import functools
+
 import jax
 import jax.numpy as jnp
 from jax import lax
+from jax.experimental import pallas as pl
+from jax.experimental.pallas import tpu as pltpu
 from jax.sharding import PartitionSpec as P
 
 
@@ -35,7 +39,7 @@
     return moved.astype(jnp.bfloat16).reshape(values.shape[0], blocks * width)
 
 
-def on_device(anomalies, innovations, sort_order, obs_error):
+def plain_on_device(anomalies, innovations, sort_order, obs_error):
     raw_y, raw_d = (
         lax.all_to_all(anomalies, "obs", split_axis=1, concat_axis=0, tiled=True),
         lax.all_to_all(innovations, "obs", split_axis=1, concat_axis=0, tiled=True),
@@ -79,9 +83,379 @@
     return total + obs_error[:, None] * d_here.T.astype(jnp.float32)
 
 
+TILE = 256
+SORT = 128
+MESH = pl.DeviceIdType.MESH
+NT = (((1,), (1,)), ((), ()))
+NN = (((1,), (0,)), ((), ()))
+
+
+def mm(a, b, dims=NN):
+    return lax.dot_general(a, b, dims, preferred_element_type=jnp.float32)
+
+
+def kernel(
+    n,
+    y_hbm, d_hbm, order_hbm, err_hbm, out_ref,
+    raw, y_ext, d_ext, y_t, weights, table, orders, errs, sel, sel_t, err_col,
+    send_sem, recv_sem, own_sem, far_send, far_recv, swap_send, swap_recv,
+    mate_send, mate_recv, order_sem, small_sem,
+):
+    me = lax.axis_index("obs")
+    rows = y_hbm.shape[0]
+    panel = y_hbm.shape[1] // n
+    members = rows * n
+    tiles = panel // TILE
+    half = n // 2
+    odd, side = me % 2, (me // 2) % 2
+    mine = (me // 4) * 2 + odd
+    own_slot = 1 - odd
+    partner = me + 2 * odd - 1
+    mate = me + 1 - 2 * odd
+    has_low, has_up = me > 0, me < n - 1
+    has_partner = (me > 0) & (me < n - 1)
+    no_partner = (me == 0) | (me == n - 1)
+    chunks = [(0, 0), (0, 1), (1, 0), (1, 1)]
+
+    def here(slot):
+        return has_low if slot == 0 else has_up
+
+    def device_at(which, j):
+        return (j // 2) * 4 + which * 2 + j % 2
+
+    barrier = pltpu.get_barrier_semaphore()
+    for k in range(1, n):
+        pl.semaphore_signal(
+            barrier, inc=1, device_id={"obs": lax.rem(me + k, n)}, device_id_type=MESH
+        )
+    pl.semaphore_wait(barrier, n - 1)
+
+    def pair_panel(owner, slot):
+        return owner - 1 + owner % 2 + slot
+
+    def columns(at):
+        return pl.ds(pl.multiple_of(at * panel, TILE), panel)
+
+    def landing(a, slot, source):
+        return raw.at[a, source // 4, (source // 2) % 2, source % 2, :, columns(slot)]
+
+    def side_copy(i, k, owner, source):
+        a, slot = chunks[i]
+        return pltpu.make_async_remote_copy(
+            src_ref=(y_hbm, d_hbm)[a].at[:, columns(pair_panel(owner, slot))],
+            dst_ref=landing(a, slot, source),
+            send_sem=send_sem.at[i, k],
+            recv_sem=recv_sem.at[i, k],
+            device_id={"obs": owner},
+            device_id_type=MESH,
+        )
+
+    def own_copy(i):
+        a, slot = chunks[i]
+        return pltpu.make_async_copy(
+            (y_hbm, d_hbm)[a].at[:, columns(pair_panel(me, slot))],
+            landing(a, slot, me),
+            own_sem.at[i],
+        )
+
+    def far_copy(a, owner, source, j):
+        return pltpu.make_async_remote_copy(
+            src_ref=(y_hbm, d_hbm)[a].at[:, columns(owner)],
+            dst_ref=landing(a, 1 - owner % 2, source),
+            send_sem=far_send.at[a],
+            recv_sem=far_recv.at[a, j],
+            device_id={"obs": owner},
+            device_id_type=MESH,
+        )
+
+    def swap_copy(i, which):
+        a, slot = chunks[i]
+        part = raw.at[a, :, which, :, :, columns(slot)]
+        return pltpu.make_async_remote_copy(
+            src_ref=part,
+            dst_ref=part,
+            send_sem=swap_send.at[i],
+            recv_sem=swap_recv.at[i],
+            device_id={"obs": partner},
+            device_id_type=MESH,
+        )
+
+    def mate_copy(a, parity):
+        ext = (y_ext, d_ext)[a]
+        there = columns(2 * parity)
+        if a == 0:
+            src, dst = ext.at[:, pl.ds(panel, panel)], ext.at[:, there]
+        else:
+            src, dst = ext.at[pl.ds(panel, panel)], ext.at[there]
+        return pltpu.make_async_remote_copy(
+            src_ref=src,
+            dst_ref=dst,
+            send_sem=mate_send.at[a],
+            recv_sem=mate_recv.at[a],
+            device_id={"obs": mate},
+            device_id_type=MESH,
+        )
+
+    def order_copy(slot):
+        return pltpu.make_async_remote_copy(
+            src_ref=order_hbm,
+            dst_ref=orders.at[slot],
+            send_sem=order_sem.at[0],
+            recv_sem=order_sem.at[1],
+            device_id={"obs": partner},
+            device_id_type=MESH,
+        )
+
+    far_owner = (1 - side) * (n - 1)
+    steps = [half // 2]
+    for step in range(1, half // 2):
+        steps += [half // 2 + step, half // 2 - step]
+
+    order_here = pltpu.make_async_copy(order_hbm, orders.at[own_slot], small_sem.at[0])
+    err_here = pltpu.make_async_copy(err_hbm, errs, small_sem.at[1])
+    order_here.start()
+    err_here.start()
+
+    @pl.when(has_partner)
+    def _():
+        order_copy(own_slot).start()
+
+    def for_targets(i, act):
+        for k in steps:
+            owner = device_at(side, lax.rem(mine + k, half))
+            if chunks[i][1] == 0:
+                @pl.when(owner > 0)
+                def _():
+                    act(side_copy(i, k, owner, me))
+            else:
+                @pl.when(owner < n - 1)
+                def _():
+                    act(side_copy(i, k, owner, me))
+
+    for i, (a, slot) in enumerate(chunks):
+        for_targets(i, lambda copy: copy.start())
+
+        @pl.when(here(slot))
+        def _():
+            own_copy(i).start()
+
+        if slot == 1:
+            far_copy(a, far_owner, me, mine).start()
+
+    row_id = lax.broadcasted_iota(jnp.int32, (SORT, SORT), 0)
+    col_id = lax.broadcasted_iota(jnp.int32, (SORT, SORT), 1)
+    err_here.wait()
+    for b in range(panel // SORT):
+        err = jnp.broadcast_to(errs[b : b + 1, :], (SORT, SORT))
+        column = jnp.sum(jnp.where(row_id == col_id, err, 0.0), axis=1, keepdims=True)
+        err_col[b * SORT : (b + 1) * SORT, :] = jnp.broadcast_to(column, (SORT, SORT))
+    r = lax.broadcasted_iota(jnp.int32, (TILE, TILE), 0)
+    s = lax.broadcasted_iota(jnp.int32, (TILE, TILE), 1)
+    for j in range(2 * tiles + 1):
+        dist = jnp.abs(s - r + (j - tiles) * TILE).astype(jnp.float32)
+        table[:, j * TILE : (j + 1) * TILE] = gaspari(dist / (panel // 2 * 1.0)) / (
+            members - 1.0
+        )
+    order_here.wait()
+
+    @pl.when(has_partner)
+    def _():
+        order_copy(1 - own_slot).wait_recv()
+
+    for slot in range(2):
+        @pl.when(here(slot))
+        def _():
+            for b in range(panel // SORT):
+                ids = jnp.broadcast_to(orders[slot, b : b + 1, :] & (SORT - 1), (SORT, SORT))
+                pick = (row_id == ids).astype(jnp.float32)
+                sel[slot, b] = pick.astype(jnp.bfloat16)
+                sel_t[slot, b] = pick.T.astype(jnp.bfloat16)
+
+    def make_weights(j):
+        for t in range(tiles):
+            at = j - t
+            if 0 <= at <= 2 * tiles:
+                cols = slice(at * TILE, (at + 1) * TILE)
+                gram = mm(y_t[t * TILE : (t + 1) * TILE, :], y_ext[:, j * TILE : (j + 1) * TILE])
+                weights[t, :, cols] = (gram * table[:, cols]).astype(jnp.bfloat16)
+
+    def weights_of(first, last):
+        for j in range(first, last):
+            make_weights(j)
+
+    def apply_weights(first, last):
+        for t in range(tiles):
+            lo, hi = max(first, t), min(last, t + 2 * tiles + 1)
+            if lo < hi:
+                term = mm(
+                    weights[t, :, (lo - t) * TILE : (hi - t) * TILE],
+                    d_ext[lo * TILE : hi * TILE, :],
+                )
+                rows_here = slice(t * TILE, (t + 1) * TILE)
+                out_ref[rows_here, :] = out_ref[rows_here, :] + term
+
+    def of_partner(act):
+        @pl.when((odd == 1) & has_up)
+        def _():
+            act(2 * tiles, 3 * tiles)
+
+        @pl.when((odd == 0) & has_low)
+        def _():
+            act(0, tiles)
+
+    def of_mate(act):
+        @pl.when(odd == 1)
+        def _():
+            act(0, tiles)
+
+        @pl.when(odd == 0)
+        def _():
+            act(2 * tiles, 3 * tiles)
+
+    def gather(i):
+        a, slot = chunks[i]
+
+        @pl.when(here(slot))
+        def _():
+            own_copy(i).wait()
+            for k in steps:
+                source = device_at(side, lax.rem(mine + half - k, half))
+                side_copy(i, k, me, source).wait_recv()
+
+        @pl.when(has_partner)
+        def _():
+            swap_copy(i, side).start()
+
+    def sort_chunk(i):
+        a, slot = chunks[i]
+
+        @pl.when(has_partner)
+        def _():
+            swap_copy(i, 1 - side).wait_recv()
+
+        @pl.when(no_partner & (own_slot == slot))
+        def _():
+            for j in range(half):
+                far_copy(a, me, device_at(1 - side, j), j).wait_recv()
+
+        @pl.when(here(slot))
+        def _():
+            for b in range(panel // SORT):
+                at = slice(slot * panel + b * SORT, slot * panel + (b + 1) * SORT)
+                block = raw[a, :, :, :, :, at].reshape(members, SORT)
+                start = pl.multiple_of((odd + slot) * panel + b * SORT, SORT)
+                if a == 0:
+                    y_ext[:, pl.ds(start, SORT)] = mm(block, sel[slot, b]).astype(jnp.bfloat16)
+                else:
+                    d_ext[pl.ds(start, SORT), :] = mm(sel_t[slot, b], block, NT).astype(
+                        jnp.bfloat16
+                    )
+
+        @pl.when(own_slot == slot)
+        def _():
+            mate_copy(a, odd).start()
+            for b in range(panel // SORT):
+                cols = slice(b * SORT, (b + 1) * SORT)
+                if a == 0:
+                    at = slice(slot * panel + b * SORT, slot * panel + (b + 1) * SORT)
+                    block = raw[a, :, :, :, :, at].reshape(members, SORT)
+                    y_t[cols, :] = mm(sel_t[slot, b], block, NT).astype(jnp.bfloat16)
+                else:
+                    own = d_ext[panel + b * SORT : panel + (b + 1) * SORT, :]
+                    out_ref[cols, :] = err_col[cols, 0:1] * own.astype(jnp.float32)
+
+    gather(0)
+    gather(1)
+    sort_chunk(0)
+    gather(2)
+    sort_chunk(1)
+    weights_of(tiles, 2 * tiles)
+    of_partner(weights_of)
+    gather(3)
+    mate_copy(0, 1 - odd).wait_recv()
+    of_mate(weights_of)
+    sort_chunk(2)
+    sort_chunk(3)
+    apply_weights(tiles, 2 * tiles)
+    of_partner(apply_weights)
+    mate_copy(1, 1 - odd).wait_recv()
+    of_mate(apply_weights)
+
+    for i, (a, slot) in enumerate(chunks):
+        for_targets(i, lambda copy: copy.wait_send())
+        if slot == 1:
+            far_copy(a, far_owner, me, mine).wait_send()
+            mate_copy(a, odd).wait_send()
+
+        @pl.when(has_partner)
+        def _():
+            swap_copy(i, side).wait_send()
+
+    @pl.when(has_partner)
+    def _():
+        order_copy(own_slot).wait_send()
+
+
+def fused_on_device(n, anomalies, innovations, sort_order, obs_error):
+    rows, total = anomalies.shape
+    panel = total // n
+    members = rows * n
+    tiles = panel // TILE
+    blocks = panel // SORT
+    half = n // 2
+    bf16, f32 = jnp.bfloat16, jnp.float32
+    hbm = pl.BlockSpec(memory_space=pltpu.HBM)
+    dma = pltpu.SemaphoreType.DMA
+    return pl.pallas_call(
+        functools.partial(kernel, n),
+        out_shape=jax.ShapeDtypeStruct((panel, members), f32),
+        in_specs=[hbm] * 4,
+        out_specs=pl.BlockSpec(memory_space=pltpu.VMEM),
+        scratch_shapes=[
+            pltpu.VMEM((2, n // 4, 2, 2, rows, 2 * panel), bf16),
+            pltpu.VMEM((members, 3 * panel), bf16),
+            pltpu.VMEM((3 * panel, members), bf16),
+            pltpu.VMEM((panel, members), bf16),
+            pltpu.VMEM((tiles, TILE, (2 * tiles + 1) * TILE), bf16),
+            pltpu.VMEM((TILE, (2 * tiles + 1) * TILE), f32),
+            pltpu.VMEM((2, blocks, SORT), jnp.int32),
+            pltpu.VMEM((blocks, SORT), f32),
+            pltpu.VMEM((2, blocks, SORT, SORT), bf16),
+            pltpu.VMEM((2, blocks, SORT, SORT), bf16),
+            pltpu.VMEM((panel, SORT), f32),
+            dma((4, half)),
+            dma((4, half)),
+            dma((4,)),
+            dma((2,)),
+            dma((2, half)),
+            dma((4,)),
+            dma((4,)),
+            dma((2,)),
+            dma((2,)),
+            dma((2,)),
+            dma((2,)),
+        ],
+        compiler_params=pltpu.CompilerParams(
+            collective_id=0, has_side_effects=True, vmem_limit_bytes=48 * 1024 * 1024
+        ),
+    )(
+        anomalies,
+        innovations,
+        sort_order.reshape(blocks, SORT),
+        obs_error.reshape(blocks, SORT),
+    )
+
+
+def on_device(n, anomalies, innovations, sort_order, obs_error):
+    rows, total = anomalies.shape
+    if n % 4 or rows % 16 or (total // n) % (2 * TILE) or (rows * n) % TILE:
+        return plain_on_device(anomalies, innovations, sort_order, obs_error)
+    return fused_on_device(n, anomalies, innovations, sort_order, obs_error)
+
+
 def solution(mesh):
     return jax.shard_map(
-        on_device,
+        functools.partial(on_device, mesh.shape["obs"]),
         mesh=mesh,
         in_specs=(
             P(("grp", "obs"), None),

time: 76.6 us -> 49.8 us (0.65)
  Pallas kernels: 0 us -> 44.4 us
  waiting for transfers between devices: 25.3 us -> 0 us
  matrix products: 24 us -> 0 us
  starting transfers between devices: 22.5 us -> 0 us
  local copies, waits for them, and re-layouts: 2.97 us -> 4.43 us
  other arithmetic: 1.21 us -> 0 us
    pallas_call x0 -> x1, Pallas kernels: none -> 44.4 us  [fused_on_device(): pl.pallas_call(functools.partial(kernel, n), out_shape=jax.ShapeDtypeStru...]
    dot_general x8 -> x0, matrix products: 24 us -> none  [the longest x6 23.3 us: apply_rows(): lax.dot_general(weights, d_cols, (((1,), (1,)), ((), ())), preferred_elem...]
    all_to_all x2 -> x0, waiting for transfers between devices: 20 us -> none  [the longest x1 12.6 us: on_device(): lax.all_to_all(innovations, 'obs', split_axis=1, concat_axis=0, tiled=True)]
    all_to_all x2 -> x0, starting transfers between devices: 11.4 us -> none  [the longest x1 6.24 us: on_device(): lax.all_to_all(innovations, 'obs', split_axis=1, concat_axis=0, tiled=True)]
    ppermute x4 -> x0, starting transfers between devices: 11.1 us -> none  [shifted(): return lax.ppermute(shard, axis, pairs)]
    ppermute x4 -> x0, waiting for transfers between devices: 5.34 us -> none  [shifted(): return lax.ppermute(shard, axis, pairs)]
    unnamed x10 -> x9, local copies, waits for them, and re-layouts: 0.2 us -> 4.43 us
    all_to_all x2 -> x0, local copies, waits for them, and re-layouts: 2.77 us -> none  [the longest x1 1.93 us: on_device(): lax.all_to_all(innovations, 'obs', split_axis=1, concat_axis=0, tiled=True)]
  transfers between devices with their start and end apart: 6 -> 0, of which waited for: 3 -> 0; matrix products, arithmetic and copies ran while one was open for 22% -> 0% of each run, Pallas kernels for 0% -> 0%
where the time goes in v2:
time: 49.8 us; the launch traced here: 48.9 us
  Pallas kernels  44.4 us (89%)
  local copies, waits for them, and re-layouts  4.43 us (9%)
    pallas_call x1, Pallas kernels, fused_on_device(): pl.pallas_call(functools.partial(kernel, n), out_shape=jax.ShapeDtypeStru...  44.4 us
    unnamed x9, local copies, waits for them, and re-layouts  4.43 us

profile of v2, /device:TPU:14, one launch (start us, length us, event | category | flops | bytes accessed | tf_op | source)
XLA Modules:
  0.0 48.9 jit_solution(15973446758384878754)
XLA Ops:
  0.0 0.0 copy-start
  0.0 1.0 %copy-done = bf16[16,16384]{1,0:T(8,128)(2,1)S(1)} copy-done((bf16[16,16384]{1,0:T(8,128)(2,1)S(1)}, bf16[16,16384]{1,0:T(8,128)(2,1)}, u32[]{:S(2)}) %copy-start) | copy-done | bytes 524312
  1.0 0.0 copy-start.1
  1.0 1.0 %copy-done.1 = bf16[16,16384]{1,0:T(8,128)(2,1)S(1)} copy-done((bf16[16,16384]{1,0:T(8,128)(2,1)S(1)}, bf16[16,16384]{1,0:T(8,128)(2,1)}, u32[]{:S(2)}) %copy-start.1) | copy-done | bytes 524312
  2.1 0.0 copy-start.2
  2.1 0.7 %copy-done.2 = s32[1024]{0:T(1024)S(1)} copy-done((s32[1024]{0:T(1024)S(1)}, s32[1024]{0:T(1024)}, u32[]{:S(2)}) %copy-start.2) | copy-done | bytes 4120
  2.8 0.0 copy-start.3
  2.8 0.7 %copy-done.3 = f32[1024]{0:T(1024)S(1)} copy-done((f32[1024]{0:T(1024)S(1)}, f32[1024]{0:T(1024)}, u32[]{:S(2)}) %copy-start.3) | copy-done | bytes 4120
  3.5 44.4 %shard_map.46 = f32[1024,256]{1,0:T(8,128)S(1)} custom-call(bf16[16,16384]{1,0:T(8,128)(2,1)S(1)} %copy-done, bf16[16,16384]{1,0:T(8,128)(2,1)S(1)} %copy-done.1, s32[8,128]{1,0:T(8,128)S(1)} %bitcast.2, f32[8,128]{1,0:T(8,128)S(1)} %bitcast.3), custom_call_target="tpu_custom_call" | custom-call | tf_op jit(solution)/shard_map/pallas_call | solution.py:409
  47.9 1.0 %copy.6 = f32[1024,256]{1,0:T(8,128)} copy(f32[1024,256]{1,0:T(8,128)S(1)} %shard_map.46) | data formatting | bytes 2097152
Async XLA Ops:
  0.0 1.0 %copy-start = (bf16[16,16384]{1,0:T(8,128)(2,1)S(1)}, bf16[16,16384]{1,0:T(8,128)(2,1)}, u32[]{:S(2)}) copy-start(bf16[16,16384]{1,0:T(8,128)(2,1)} %y_hbm.1) | copy-start | bytes 1572868
  1.0 1.0 %copy-start.1 = (bf16[16,16384]{1,0:T(8,128)(2,1)S(1)}, bf16[16,16384]{1,0:T(8,128)(2,1)}, u32[]{:S(2)}) copy-start(bf16[16,16384]{1,0:T(8,128)(2,1)} %d_hbm.1) | copy-start | bytes 1572868
  2.1 0.7 %copy-start.2 = (s32[1024]{0:T(1024)S(1)}, s32[1024]{0:T(1024)}, u32[]{:S(2)}) copy-start(s32[1024]{0:T(1024)} %param.6) | copy-start | bytes 12292
  2.8 0.7 %copy-start.3 = (f32[1024]{0:T(1024)S(1)}, f32[1024]{0:T(1024)}, u32[]{:S(2)}) copy-start(f32[1024]{0:T(1024)} %param.7) | copy-start | bytes 12292

commit v3 on v2

--- a/solution.py
+++ b/solution.py
@@ -232,7 +232,8 @@
                 def _():
                     act(side_copy(i, k, owner, me))
 
-    for i, (a, slot) in enumerate(chunks):
+    def start_chunk(i):
+        a, slot = chunks[i]
         for_targets(i, lambda copy: copy.start())
 
         @pl.when(here(slot))
@@ -241,6 +242,9 @@
 
         if slot == 1:
             far_copy(a, far_owner, me, mine).start()
+
+    start_chunk(0)
+    start_chunk(1)
 
     row_id = lax.broadcasted_iota(jnp.int32, (SORT, SORT), 0)
     col_id = lax.broadcasted_iota(jnp.int32, (SORT, SORT), 1)
@@ -249,13 +253,6 @@
         err = jnp.broadcast_to(errs[b : b + 1, :], (SORT, SORT))
         column = jnp.sum(jnp.where(row_id == col_id, err, 0.0), axis=1, keepdims=True)
         err_col[b * SORT : (b + 1) * SORT, :] = jnp.broadcast_to(column, (SORT, SORT))
-    r = lax.broadcasted_iota(jnp.int32, (TILE, TILE), 0)
-    s = lax.broadcasted_iota(jnp.int32, (TILE, TILE), 1)
-    for j in range(2 * tiles + 1):
-        dist = jnp.abs(s - r + (j - tiles) * TILE).astype(jnp.float32)
-        table[:, j * TILE : (j + 1) * TILE] = gaspari(dist / (panel // 2 * 1.0)) / (
-            members - 1.0
-        )
     order_here.wait()
 
     @pl.when(has_partner)
@@ -270,6 +267,15 @@
                 pick = (row_id == ids).astype(jnp.float32)
                 sel[slot, b] = pick.astype(jnp.bfloat16)
                 sel_t[slot, b] = pick.T.astype(jnp.bfloat16)
+
+    def make_table():
+        r = lax.broadcasted_iota(jnp.int32, (TILE, TILE), 0)
+        s = lax.broadcasted_iota(jnp.int32, (TILE, TILE), 1)
+        for j in range(2 * tiles + 1):
+            dist = jnp.abs(s - r + (j - tiles) * TILE).astype(jnp.float32)
+            table[:, j * TILE : (j + 1) * TILE] = gaspari(dist / (panel // 2 * 1.0)) / (
+                members - 1.0
+            )
 
     def make_weights(j):
         for t in range(tiles):
@@ -365,7 +371,10 @@
                     out_ref[cols, :] = err_col[cols, 0:1] * own.astype(jnp.float32)
 
     gather(0)
+    start_chunk(2)
+    make_table()
     gather(1)
+    start_chunk(3)
     sort_chunk(0)
     gather(2)
     sort_chunk(1)
@@ -436,7 +445,7 @@
             dma((2,)),
         ],
         compiler_params=pltpu.CompilerParams(
-            collective_id=0, has_side_effects=True, vmem_limit_bytes=48 * 1024 * 1024
+            collective_id=0, has_side_effects=True, vmem_limit_bytes=63 * 1024 * 1024
         ),
     )(
         anomalies,

time: 49.8 us -> 47.9 us (0.962)
  local copies, waits for them, and re-layouts: 4.43 us -> 2.26 us
    unnamed x9 -> x1, local copies, waits for them, and re-layouts: 4.43 us -> 2.26 us
where the time goes in v3:
time: 47.9 us; the launch traced here: 47 us
  Pallas kernels  44.7 us (93%)
  local copies, waits for them, and re-layouts  2.26 us (5%)
    pallas_call x1, Pallas kernels, fused_on_device(): pl.pallas_call(functools.partial(kernel, n), out_shape=jax.ShapeDtypeStru...  44.7 us
    unnamed x1, local copies, waits for them, and re-layouts  2.26 us

profile of v3, /device:TPU:14, one launch (start us, length us, event | category | flops | bytes accessed | tf_op | source)
XLA Modules:
  0.0 47.0 jit_solution(15925457477441779434)
XLA Ops:
  0.0 44.7 %shard_map.46 = f32[1024,256]{1,0:T(8,128)} custom-call(bf16[16,16384]{1,0:T(8,128)(2,1)} %y_hbm.1, bf16[16,16384]{1,0:T(8,128)(2,1)} %d_hbm.1, s32[8,128]{1,0:T(8,128)} %bitcast.2, f32[8,128]{1,0:T(8,128)} %bitcast.3), custom_call_target="tpu_custom_call" | custom-call | tf_op jit(solution)/shard_map/pallas_call | solution.py:418
  44.8 2.3 %copy.6 = f32[1024,256]{1,0:T(8,128)} copy(f32[1024,256]{1,0:T(8,128)} %shard_map.46) | data formatting | bytes 2097152

commit v4 on v3

--- a/solution.py
+++ b/solution.py
@@ -115,7 +115,10 @@
     has_low, has_up = me > 0, me < n - 1
     has_partner = (me > 0) & (me < n - 1)
     no_partner = (me == 0) | (me == n - 1)
-    chunks = [(0, 0), (0, 1), (1, 0), (1, 1)]
+    part = panel // 2
+    chunks = [(0, 0, 0, panel), (0, 1, 0, panel)] + [
+        (1, slot, first, part) for first in (0, part) for slot in range(2)
+    ]
 
     def here(slot):
         return has_low if slot == 0 else has_up
@@ -133,17 +136,18 @@
     def pair_panel(owner, slot):
         return owner - 1 + owner % 2 + slot
 
-    def columns(at):
-        return pl.ds(pl.multiple_of(at * panel, TILE), panel)
-
-    def landing(a, slot, source):
-        return raw.at[a, source // 4, (source // 2) % 2, source % 2, :, columns(slot)]
+    def columns(at, first=0, width=panel):
+        return pl.ds(pl.multiple_of(at * panel + first, TILE), width)
+
+    def landing(a, slot, source, first=0, width=panel):
+        at = columns(slot, first, width)
+        return raw.at[a, source // 4, (source // 2) % 2, source % 2, :, at]
 
     def side_copy(i, k, owner, source):
-        a, slot = chunks[i]
+        a, slot, first, width = chunks[i]
         return pltpu.make_async_remote_copy(
-            src_ref=(y_hbm, d_hbm)[a].at[:, columns(pair_panel(owner, slot))],
-            dst_ref=landing(a, slot, source),
+            src_ref=(y_hbm, d_hbm)[a].at[:, columns(pair_panel(owner, slot), first, width)],
+            dst_ref=landing(a, slot, source, first, width),
             send_sem=send_sem.at[i, k],
             recv_sem=recv_sem.at[i, k],
             device_id={"obs": owner},
@@ -151,10 +155,10 @@
         )
 
     def own_copy(i):
-        a, slot = chunks[i]
+        a, slot, first, width = chunks[i]
         return pltpu.make_async_copy(
-            (y_hbm, d_hbm)[a].at[:, columns(pair_panel(me, slot))],
-            landing(a, slot, me),
+            (y_hbm, d_hbm)[a].at[:, columns(pair_panel(me, slot), first, width)],
+            landing(a, slot, me, first, width),
             own_sem.at[i],
         )
 
@@ -169,29 +173,29 @@
         )
 
     def swap_copy(i, which):
-        a, slot = chunks[i]
-        part = raw.at[a, :, which, :, :, columns(slot)]
+        a, slot, first, width = chunks[i]
+        held = raw.at[a, :, which, :, :, columns(slot, first, width)]
         return pltpu.make_async_remote_copy(
-            src_ref=part,
-            dst_ref=part,
+            src_ref=held,
+            dst_ref=held,
             send_sem=swap_send.at[i],
             recv_sem=swap_recv.at[i],
             device_id={"obs": partner},
             device_id_type=MESH,
         )
 
-    def mate_copy(a, parity):
+    def mate_copy(a, parity, first=0, width=panel):
         ext = (y_ext, d_ext)[a]
-        there = columns(2 * parity)
+        there = columns(2 * parity, first, width)
         if a == 0:
             src, dst = ext.at[:, pl.ds(panel, panel)], ext.at[:, there]
         else:
-            src, dst = ext.at[pl.ds(panel, panel)], ext.at[there]
+            src, dst = ext.at[pl.ds(panel + first, width)], ext.at[there]
         return pltpu.make_async_remote_copy(
             src_ref=src,
             dst_ref=dst,
-            send_sem=mate_send.at[a],
-            recv_sem=mate_recv.at[a],
+            send_sem=mate_send.at[a, first // part],
+            recv_sem=mate_recv.at[a, first // part],
             device_id={"obs": mate},
             device_id_type=MESH,
         )
@@ -233,18 +237,19 @@
                     act(side_copy(i, k, owner, me))
 
     def start_chunk(i):
-        a, slot = chunks[i]
+        a, slot, first, width = chunks[i]
         for_targets(i, lambda copy: copy.start())
 
         @pl.when(here(slot))
         def _():
             own_copy(i).start()
 
-        if slot == 1:
+        if slot == 1 and first == 0:
             far_copy(a, far_owner, me, mine).start()
 
     start_chunk(0)
     start_chunk(1)
+    start_chunk(2)
 
     row_id = lax.broadcasted_iota(jnp.int32, (SORT, SORT), 0)
     col_id = lax.broadcasted_iota(jnp.int32, (SORT, SORT), 1)
@@ -319,7 +324,7 @@
             act(2 * tiles, 3 * tiles)
 
     def gather(i):
-        a, slot = chunks[i]
+        a, slot, first, width = chunks[i]
 
         @pl.when(here(slot))
         def _():
@@ -333,7 +338,7 @@
             swap_copy(i, side).start()
 
     def sort_chunk(i):
-        a, slot = chunks[i]
+        a, slot, first, width = chunks[i]
 
         @pl.when(has_partner)
         def _():
@@ -341,12 +346,13 @@
 
         @pl.when(no_partner & (own_slot == slot))
         def _():
-            for j in range(half):
-                far_copy(a, me, device_at(1 - side, j), j).wait_recv()
+            if first == 0:
+                for j in range(half):
+                    far_copy(a, me, device_at(1 - side, j), j).wait_recv()
 
         @pl.when(here(slot))
         def _():
-            for b in range(panel // SORT):
+            for b in range(first // SORT, (first + width) // SORT):
                 at = slice(slot * panel + b * SORT, slot * panel + (b + 1) * SORT)
                 block = raw[a, :, :, :, :, at].reshape(members, SORT)
                 start = pl.multiple_of((odd + slot) * panel + b * SORT, SORT)
@@ -359,8 +365,8 @@
 
         @pl.when(own_slot == slot)
         def _():
-            mate_copy(a, odd).start()
-            for b in range(panel // SORT):
+            mate_copy(a, odd, first, width).start()
+            for b in range(first // SORT, (first + width) // SORT):
                 cols = slice(b * SORT, (b + 1) * SORT)
                 if a == 0:
                     at = slice(slot * panel + b * SORT, slot * panel + (b + 1) * SORT)
@@ -371,30 +377,35 @@
                     out_ref[cols, :] = err_col[cols, 0:1] * own.astype(jnp.float32)
 
     gather(0)
-    start_chunk(2)
+    start_chunk(3)
     make_table()
     gather(1)
-    start_chunk(3)
+    start_chunk(4)
     sort_chunk(0)
     gather(2)
+    start_chunk(5)
     sort_chunk(1)
     weights_of(tiles, 2 * tiles)
+    gather(3)
     of_partner(weights_of)
-    gather(3)
+    gather(4)
     mate_copy(0, 1 - odd).wait_recv()
     of_mate(weights_of)
-    sort_chunk(2)
-    sort_chunk(3)
+    gather(5)
+    for i in range(2, 6):
+        sort_chunk(i)
     apply_weights(tiles, 2 * tiles)
     of_partner(apply_weights)
-    mate_copy(1, 1 - odd).wait_recv()
+    for first in (0, part):
+        mate_copy(1, 1 - odd, first, part).wait_recv()
     of_mate(apply_weights)
 
-    for i, (a, slot) in enumerate(chunks):
+    for i, (a, slot, first, width) in enumerate(chunks):
         for_targets(i, lambda copy: copy.wait_send())
         if slot == 1:
-            far_copy(a, far_owner, me, mine).wait_send()
-            mate_copy(a, odd).wait_send()
+            mate_copy(a, odd, first, width).wait_send()
+            if first == 0:
+                far_copy(a, far_owner, me, mine).wait_send()
 
         @pl.when(has_partner)
         def _():
@@ -432,20 +443,20 @@
             pltpu.VMEM((2, blocks, SORT, SORT), bf16),
             pltpu.VMEM((2, blocks, SORT, SORT), bf16),
             pltpu.VMEM((panel, SORT), f32),
-            dma((4, half)),
-            dma((4, half)),
-            dma((4,)),
+            dma((6, half)),
+            dma((6, half)),
+            dma((6,)),
             dma((2,)),
             dma((2, half)),
-            dma((4,)),
-            dma((4,)),
-            dma((2,)),
-            dma((2,)),
+            dma((6,)),
+            dma((6,)),
+            dma((2, 2)),
+            dma((2, 2)),
             dma((2,)),
             dma((2,)),
         ],
         compiler_params=pltpu.CompilerParams(
-            collective_id=0, has_side_effects=True, vmem_limit_bytes=63 * 1024 * 1024
+            collective_id=0, has_side_effects=True, vmem_limit_bytes=64512 * 1024
         ),
     )(
         anomalies,

time: 47.9 us -> 48.8 us (1.019)
  Pallas kernels: 44.7 us -> 46 us
    pallas_call x1, Pallas kernels: 44.7 us -> 46 us  [fused_on_device(): pl.pallas_call(functools.partial(kernel, n), out_shape=jax.ShapeDtypeStru...]
where the time goes in v4:
time: 48.8 us; the launch traced here: 48.2 us
  Pallas kernels  46 us (94%)
  local copies, waits for them, and re-layouts  2.26 us (5%)
    pallas_call x1, Pallas kernels, fused_on_device(): pl.pallas_call(functools.partial(kernel, n), out_shape=jax.ShapeDtypeStru...  46 us
    unnamed x1, local copies, waits for them, and re-layouts  2.26 us

profile of v4, /device:TPU:14, one launch (start us, length us, event | category | flops | bytes accessed | tf_op | source)
XLA Modules:
  0.0 48.2 jit_solution(396996974487978438)
XLA Ops:
  0.0 46.0 %shard_map.46 = f32[1024,256]{1,0:T(8,128)} custom-call(bf16[16,16384]{1,0:T(8,128)(2,1)} %y_hbm.1, bf16[16,16384]{1,0:T(8,128)(2,1)} %d_hbm.1, s32[8,128]{1,0:T(8,128)} %bitcast.2, f32[8,128]{1,0:T(8,128)} %bitcast.3), custom_call_target="tpu_custom_call" | custom-call | tf_op jit(solution)/shard_map/pallas_call | solution.py:429
  46.0 2.3 %copy.6 = f32[1024,256]{1,0:T(8,128)} copy(f32[1024,256]{1,0:T(8,128)} %shard_map.46) | data formatting | bytes 2097152

commit v5 on v3

--- a/solution.py
+++ b/solution.py
@@ -245,6 +245,7 @@
 
     start_chunk(0)
     start_chunk(1)
+    start_chunk(2)
 
     row_id = lax.broadcasted_iota(jnp.int32, (SORT, SORT), 0)
     col_id = lax.broadcasted_iota(jnp.int32, (SORT, SORT), 1)
@@ -371,10 +372,9 @@
                     out_ref[cols, :] = err_col[cols, 0:1] * own.astype(jnp.float32)
 
     gather(0)
-    start_chunk(2)
+    start_chunk(3)
     make_table()
     gather(1)
-    start_chunk(3)
     sort_chunk(0)
     gather(2)
     sort_chunk(1)

time: 47.9 us -> 48.6 us (1.015)
  Pallas kernels: 44.7 us -> 45.4 us
    pallas_call x1, Pallas kernels: 44.7 us -> 45.4 us  [fused_on_device(): pl.pallas_call(functools.partial(kernel, n), out_shape=jax.ShapeDtypeStru...]
where the time goes in v5:
time: 48.6 us; the launch traced here: 47.7 us
  Pallas kernels  45.4 us (93%)
  local copies, waits for them, and re-layouts  2.26 us (5%)
    pallas_call x1, Pallas kernels, fused_on_device(): pl.pallas_call(functools.partial(kernel, n), out_shape=jax.ShapeDtypeStru...  45.4 us
    unnamed x1, local copies, waits for them, and re-layouts  2.26 us

profile of v5, /device:TPU:14, one launch (start us, length us, event | category | flops | bytes accessed | tf_op | source)
XLA Modules:
  0.0 47.7 jit_solution(17752593557057997734)
XLA Ops:
  0.0 45.4 %shard_map.46 = f32[1024,256]{1,0:T(8,128)} custom-call(bf16[16,16384]{1,0:T(8,128)(2,1)} %y_hbm.1, bf16[16,16384]{1,0:T(8,128)(2,1)} %d_hbm.1, s32[8,128]{1,0:T(8,128)} %bitcast.2, f32[8,128]{1,0:T(8,128)} %bitcast.3), custom_call_target="tpu_custom_call" | custom-call | tf_op jit(solution)/shard_map/pallas_call | solution.py:418
  45.4 2.3 %copy.6 = f32[1024,256]{1,0:T(8,128)} copy(f32[1024,256]{1,0:T(8,128)} %shard_map.46) | data formatting | bytes 2097152
